TPU v7x, 512 devices: a whole 4x8x8 slice. The times are simulated.
512 devices in a mesh: dp: 16 (over y, core), fsdp: 32 (over x, z).
Axes of the slice: x: 4, y: 8, z: 8, core: 2. Of those that a mesh axis runs over, the one named last changes fastest.
Arguments:
- tokens: bfloat16 [49152, 8192], P('dp', 'fsdp'), may hold values from -6 to 6
- cotangent: bfloat16 [49152, 8192], P('dp', 'fsdp'), may hold values from -0.02734375 to 0.02734375
- projection: bfloat16 [8192, 512], P('fsdp'), may hold values from -0.0625 to 0.0625
- weight: bfloat16 [8192, 8192], P('dp', 'fsdp'), may hold values from -0.0625 to 0.0625
- first_moment: float32 [512, 8192], P('dp', 'fsdp'), may hold values from -6 to 6
- second_moment: float32 [512, 8192], P('dp', 'fsdp'), may hold values from 0.25 to 4
Outputs:
- new_weight: bfloat16 [8192, 8192], P('dp', 'fsdp')
- new_first: float32 [512, 8192], P('dp', 'fsdp')
- new_second: float32 [512, 8192], P('dp', 'fsdp')
All inputs are finite; a program needn't handle non-finite values.
Results may differ from a plain program's by a relative error of at most 0.0065.
Values may be sent and summed in bfloat16 or wider, within the bound.
A program may use at most 64 MiB of HBM per device.

v0:
```python
import jax
import jax.numpy as jnp
from jax import lax
from jax.sharding import PartitionSpec as P

STEP = 10


BETA_ONE = 0.9
BETA_TWO = 0.999
EPSILON = 1e-08
RATE = 0.1


def shards(tokens, cotangent, projection, weight, first_moment, second_moment):
    partial_low = jnp.dot(tokens, projection, preferred_element_type=jnp.float32)
    reduced = lax.psum(partial_low.astype(jnp.bfloat16), "fsdp")
    gradient = lax.psum_scatter(
        lax.dot_general(
            reduced, cotangent, (((0,), (0,)), ((), ())), preferred_element_type=jnp.float32
        ).astype(jnp.bfloat16),
        "dp",
        scatter_dimension=0,
        tiled=True,
    ).astype(jnp.float32)
    new_first = BETA_ONE * first_moment + (1.0 - BETA_ONE) * gradient
    new_second = BETA_TWO * second_moment + (1.0 - BETA_TWO) * gradient * gradient
    first_fix = 1.0 - BETA_ONE**STEP
    second_fix = 1.0 - BETA_TWO**STEP
    direction = (new_first / first_fix / (jnp.sqrt(new_second / second_fix) + EPSILON)).astype(
        jnp.bfloat16
    )
    full_direction = lax.all_gather(direction, "dp", axis=0, tiled=True)
    weight_rows = weight.shape[0]
    gathered = lax.all_gather(projection, "fsdp", axis=0, tiled=True)
    local_rows = lax.dynamic_slice_in_dim(
        gathered, lax.axis_index("dp") * weight_rows, weight_rows, 0
    )
    update = jnp.dot(local_rows, full_direction, preferred_element_type=jnp.float32)
    new_weight = (weight.astype(jnp.float32) - RATE * update).astype(jnp.bfloat16)
    return (new_weight, new_first, new_second)


def solution(mesh):
    return jax.shard_map(
        shards,
        mesh=mesh,
        in_specs=(
            P("dp", "fsdp"),
            P("dp", "fsdp"),
            P("fsdp", None),
            P("dp", "fsdp"),
            P("dp", "fsdp"),
            P("dp", "fsdp"),
        ),
        out_specs=(P("dp", "fsdp"), P("dp", "fsdp"), P("dp", "fsdp")),
        check_vma=False,
    )
```

profile of v0, /device:TPU:1, one launch (start us, length us, event | category | flops | bytes accessed | tf_op | source)
XLA Modules:
  0.0 361.2 jit_solution(7758648152768639588)
XLA Ops:
  7.2 0.0 copy-start
  7.2 0.0 all-reduce.2.cloned.1.call-start
  7.2 1.4 copy-done
  8.6 3.6 convolution_convert_fusion
  12.2 0.0 copy-start.1
  12.2 0.0 all-reduce.2.cloned.1.call-update
  12.2 0.0 copy-start.3
  12.2 0.0 copy-start.4
  12.2 0.0 copy-start.2
  12.3 0.0 reduce-scatter.2.cloned.1.call-start
  12.3 171.5 %all-reduce.2.cloned.1.call-done = bf16[3072,512]{1,0:T(8,128)(2,1)} async-done(((bf16[3072,512]{1,0:T(8,128)(2,1)}), bf16[3072,512]{1,0:T(8,128)(2,1)}) %all-reduce.2.cloned.1.call-update) | async-done | bytes 3145744 | tf_op jit(solution)/shard_map/psum | solution.py:17
  183.8 0.0 copy-done.1
  183.8 3.6 %convolution_convert_fusion.1 = bf16[512,256]{1,0:T(8,128)(2,1)} fusion(bf16[3072,512]{1,0:T(8,128)(2,1)} %all-reduce.2.cloned.1.call-done, bf16[3072,256]{1,0:T(8,128)(2,1)S(1)} %copy-done.1), kind=kOutput, calls=%fused_computation.4 | convolution fusion | flops 805437440 | bytes 4980736 | tf_op jit(solution)/shard_map/dot_general | solution.py:19
  187.4 0.0 reduce-scatter.2.cloned.1.call-update
  187.4 0.0 all-gather.2.cloned.1.call-start
  187.4 0.7 all-gather.2.cloned.1.call-update
  188.1 56.5 %reduce-scatter.2.cloned.1.call-done = bf16[32,256]{1,0:T(8,128)(2,1)} async-done(((bf16[512,256]{1,0:T(8,128)(2,1)}), bf16[32,256]{1,0:T(8,128)(2,1)}) %reduce-scatter.2.cloned.1.call-update) | async-done | bytes 16400 | tf_op jit(solution)/shard_map/reduce_scatter | solution.py:18
  244.7 0.0 copy-done.3
  244.7 0.0 copy-done.4
  244.7 1.4 divide_convert_fusion
  246.0 17.0 %all_gather.7 = bf16[512,256]{1,0:T(8,128)(2,1)S(1)} all-gather(bf16[32,256]{1,0:T(8,128)(2,1)S(1)} %get-tuple-element.3), channel_id=1, replica_groups=mesh['dp'=16,'fsdp'=32] {'dp'}, dimensions={0}, use_global_device_ids=true | all-gather | bytes 278528 | tf_op jit(solution)/shard_map/all_gather | solution.py:33
  263.1 89.6 %all-gather.2.cloned.1.call-done = bf16[8192,512]{1,0:T(8,128)(2,1)} async-done(((bf16[256,512]{1,0:T(8,128)(2,1)}), bf16[8192,512]{1,0:T(8,128)(2,1)}) %all-gather.2.cloned.1.call-update) | async-done | bytes 8388624 | tf_op jit(solution)/shard_map/all_gather | solution.py:35
  352.7 0.0 copy-done.2
  352.7 2.0 fusion.1
Async XLA Ops:
  7.2 1.4 copy-start
  7.2 176.6 %all-reduce.2.cloned.1.call-start = ((), (), s32[]{:S(2)}) async-start(), calls=%async_computation.2 | async-start | bytes 6291456 | tf_op jit(solution)/shard_map/psum | solution.py:17
  12.2 171.6 %copy-start.1 = (bf16[3072,256]{1,0:T(8,128)(2,1)S(1)}, bf16[3072,256]{1,0:T(8,128)(2,1)}, u32[]{:S(2)}) copy-start(bf16[3072,256]{1,0:T(8,128)(2,1)} %param.7) | copy-start | bytes 4718596
  12.2 232.4 %copy-start.3 = (f32[32,256]{1,0:T(8,128)S(1)}, f32[32,256]{1,0:T(8,128)}, u32[]{:S(2)}) copy-start(f32[32,256]{1,0:T(8,128)} %param.10) | copy-start | bytes 98308
  12.2 232.4 %copy-start.4 = (f32[32,256]{1,0:T(8,128)S(1)}, f32[32,256]{1,0:T(8,128)}, u32[]{:S(2)}) copy-start(f32[32,256]{1,0:T(8,128)} %param.11) | copy-start | bytes 98308
  12.2 340.4 %copy-start.2 = (bf16[512,256]{1,0:T(8,128)(2,1)S(1)}, bf16[512,256]{1,0:T(8,128)(2,1)}, u32[]{:S(2)}) copy-start(bf16[512,256]{1,0:T(8,128)(2,1)} %param.9) | copy-start | bytes 786436
  12.3 232.4 %reduce-scatter.2.cloned.1.call-start = ((), (), s32[]{:S(2)}) async-start(), calls=%async_computation.3 | async-start | bytes 278528 | tf_op jit(solution)/shard_map/reduce_scatter | solution.py:18
  187.4 165.3 %all-gather.2.cloned.1.call-start = ((), (), s32[]{:S(2)}) async-start(), calls=%async_computation.1 | async-start | bytes 8650752 | tf_op jit(solution)/shard_map/all_gather | solution.py:35
Sparse Core Ops, SparseCore 0:
  12.3 171.3 all-reduce.1
  187.5 57.0 reduce-scatter.1
  247.8 104.7 all-gather.1
where the time goes:
time: 362 us; the launch traced here: 361 us
  waiting for transfers between devices  318 us (88%)
  blocking collectives  17 us (5%)
  between operations  13.8 us (4%)
  matrix products  9.27 us (3%)
    psum x1, waiting for transfers between devices, shards(): reduced = lax.psum(partial_low.astype(jnp.bfloat16), 'fsdp')  171 us
    all_gather x1, waiting for transfers between devices, shards(): gathered = lax.all_gather(projection, 'fsdp', axis=0, tiled=True)  89.6 us
    reduce_scatter x1, waiting for transfers between devices, shards(): lax.psum_scatter(lax.dot_general(reduced, cotangent, (((0,), (0,)), ((),...  56.5 us
    all_gather x1, blocking collectives, shards(): full_direction = lax.all_gather(direction, 'dp', axis=0, tiled=True)  17 us
  transfers between devices with their start and end apart: 3, of which 3 were waited for; matrix products, arithmetic and copies ran while one was open for 0% of the time, Pallas kernels for 0%

commit v1 on v0

v1 whole, which is shorter than its diff:
```python
import functools

import jax
import jax.numpy as jnp
from jax import lax
from jax.experimental import pallas as pl
from jax.experimental.pallas import tpu as pltpu
from jax.sharding import PartitionSpec as P

STEP = 10
BETA_ONE = 0.9
BETA_TWO = 0.999
EPSILON = 1e-08
RATE = 0.1

NX, NY, NZ = 4, 8, 8
RANK = 512
WIDTH = 256
QUARTER = 768
CHUNKS = 3
TC = QUARTER // CHUNKS
MESH = pl.DeviceIdType.MESH
F32 = jnp.float32
BF16 = jnp.bfloat16


def kernel(
    tok, cot, proj, wgt, m1, m2, nw, n1, n2,
    pt, t4, c4, psend, zr, ag, acc, gs, gc, xs, xr, ysum, ys, yr, dirb, pu1, pu2, pu3,
    lsem, pts, ptr, pcs, pcr, ts, tr, cs, cr, zs_, zr_, as_, ar_, gcs, gcr, xss, xsr, yss, ysr,
    ds_, dr_, dcs, dcr, u1s, u1r, u2s, u2r, u3s, u3r,
):
    dp = lax.axis_index("dp")
    fs = lax.axis_index("fsdp")
    y, c = dp // 2, lax.rem(dp, 2)
    x, z = fs // NZ, lax.rem(fs, NZ)
    o = 1 - c

    def px(d):
        return (dp, lax.rem(x + d + NX, NX) * NZ + z)

    def pz(d):
        return (dp, x * NZ + lax.rem(z + d + NZ, NZ))

    def py(d, other=False):
        return (lax.rem(y + d + NY, NY) * 2 + (o if other else c), fs)

    sent = []

    def put(src, dst, ssem, rsem, dev):
        cp = pltpu.make_async_remote_copy(
            src_ref=src, dst_ref=dst, send_sem=ssem, recv_sem=rsem, device_id=dev, device_id_type=MESH
        )
        cp.start()
        sent.append(cp)

    def got(dst, ssem, rsem):
        pltpu.make_async_remote_copy(
            src_ref=dst, dst_ref=dst, send_sem=ssem, recv_sem=rsem, device_id=(dp, fs), device_id_type=MESH
        ).wait_recv()

    own_t = pltpu.make_async_copy(tok.at[pl.ds(x * QUARTER, QUARTER)], t4.at[0], lsem.at[0])
    own_c = pltpu.make_async_copy(cot.at[pl.ds(x * QUARTER, QUARTER)], c4.at[0], lsem.at[1])
    own_t.start()
    own_c.start()

    barrier = pltpu.get_barrier_semaphore()
    for d in range(1, NX):
        pl.semaphore_signal(barrier, inc=1, device_id=px(d), device_id_type=MESH)
    for d in range(1, NZ):
        pl.semaphore_signal(barrier, inc=1, device_id=pz(d), device_id_type=MESH)
    for d in range(NY):
        pl.semaphore_signal(barrier, inc=1, device_id=py(d, True), device_id_type=MESH)
        if d:
            pl.semaphore_signal(barrier, inc=1, device_id=py(d), device_id_type=MESH)
    pt[0] = proj[...].T
    pu1[x] = proj[pl.ds(dp * 16, 16)]
    pl.semaphore_wait(barrier, NX - 1 + NZ - 1 + 2 * NY - 1)

    mine, theirs = pl.ds(c * 256, 256), pl.ds(o * 256, 256)
    for d in (2, 1, 3):
        put(pt.at[0, mine], pt.at[d, mine], pts.at[d], ptr.at[d], px(d))
    for d in (2, 1, 3):
        put(pu1.at[x], pu1.at[x], u1s.at[d], u1r.at[d], px(d))
    for k in range(CHUNKS):
        for d in (2, 1, 3):
            rows = pl.ds(lax.rem(x + d, NX) * QUARTER + k * TC, TC)
            put(tok.at[rows], t4.at[d, pl.ds(k * TC, TC)], ts.at[k, d], tr.at[k, d], px(d))

    for d in (1, 3, 2):
        got(pt.at[d, mine], pts.at[d], ptr.at[d])
        put(pt.at[d, mine], pt.at[d, mine], pcs.at[d], pcr.at[d], py(0, True))
    for d in (1, 3, 2):
        got(pu1.at[lax.rem(x - d + NX, NX)], u1s.at[d], u1r.at[d])
    for d in range(1, NZ):
        put(pu1, pu2.at[z], u2s.at[d], u2r.at[d], pz(d))
    pu2[z] = pu1[...]
    for d in (1, 3, 2):
        got(pt.at[d, theirs], pcs.at[d], pcr.at[d])
    own_t.wait()

    def send_cot():
        for k in range(CHUNKS):
            for d in (2, 1, 3):
                rows = pl.ds(lax.rem(x + d, NX) * QUARTER + k * TC, TC)
                put(cot.at[rows], c4.at[d, pl.ds(k * TC, TC)], cs.at[k, d], cr.at[k, d], px(d))

    def partial(k):
        rows = pl.ds(k * TC, TC)
        for d in (1, 3, 2):
            got(t4.at[d, rows], ts.at[k, d], tr.at[k, d])
        low = None
        for d in range(NX):
            part = lax.dot_general(
                pt[d], t4[d, rows], (((1,), (1,)), ((), ())), preferred_element_type=F32
            )
            low = part if low is None else low + part
        psend[k] = low.astype(BF16).reshape(NZ, RANK // NZ, TC)
        for d in (4, 3, 5, 2, 6, 1, 7):
            put(psend.at[k, lax.rem(z + d, NZ)], zr.at[k, d], zs_.at[k, d], zr_.at[k, d], pz(d))

    def reduce(k):
        total = psend[k, z].astype(F32)
        for d in (1, 7, 2, 6, 3, 5, 4):
            got(zr.at[k, d], zs_.at[k, d], zr_.at[k, d])
            total = total + zr[k, d].astype(F32)
        ag[k, z] = total.astype(BF16)
        for d in (4, 3, 5, 2, 6, 1, 7):
            put(ag.at[k, z], ag.at[k, z], as_.at[k, d], ar_.at[k, d], pz(d))

    def send_update_rows():
        for d in range(1, NZ):
            got(pu2.at[lax.rem(z - d + NZ, NZ)], u2s.at[d], u2r.at[d])
        for d in range(NY):
            for e in range(2):
                peer = lax.rem(y + d, NY) * 2 + (o if e else c)
                src = pu2.at[pl.ds(2 * lax.rem(peer, 4), 2), peer // 4]
                if d == 0 and e == 0:
                    pu3[:, dp] = pu2[pl.ds(2 * lax.rem(peer, 4), 2), peer // 4]
                else:
                    put(src, pu3.at[:, dp], u3s.at[d, e], u3r.at[d, e], py(d, e == 1))

    for k in range(CHUNKS):
        partial(k)
        if k == CHUNKS - 2:
            send_cot()
        if k >= 1:
            reduce(k - 1)
        if k == 0:
            send_update_rows()
    reduce(CHUNKS - 1)

    own_c.wait()
    for k in range(CHUNKS):
        rows = pl.ds(k * TC, TC)
        for d in (1, 7, 2, 6, 3, 5, 4):
            got(ag.at[k, lax.rem(z - d + NZ, NZ)], as_.at[k, d], ar_.at[k, d])
        low = ag[k].reshape(RANK, TC)
        for d in (0, 1, 3, 2):
            if d:
                got(c4.at[d, rows], cs.at[k, d], cr.at[k, d])
            part = jnp.dot(low, c4[d, rows], preferred_element_type=F32).reshape(NY, 2, 32, WIDTH)
            acc[d] = part if k == 0 else acc[d] + part

    for d in (2, 1, 3, 0):
        gs[d] = acc[d, :, o].astype(BF16)
        put(gs.at[d], gc.at[d], gcs.at[d], gcr.at[d], py(0, True))
    for d in (2, 1, 3):
        got(gc.at[d], gcs.at[d], gcr.at[d])
        xs[d] = (acc[d, :, c] + gc[d].astype(F32)).astype(BF16)
        put(xs.at[d], xr.at[d], xss.at[d], xsr.at[d], px(-d))
    got(gc.at[0], gcs.at[0], gcr.at[0])
    total = acc[0, :, c] + gc[0].astype(F32)
    for d in (1, 3, 2):
        got(xr.at[d], xss.at[d], xsr.at[d])
        total = total + xr[d].astype(F32)
    ysum[...] = total
    ys[...] = total.astype(BF16)
    for d in (4, 3, 5, 2, 6, 1, 7):
        put(ys.at[lax.rem(y + d, NY)], yr.at[d], yss.at[d], ysr.at[d], py(d))
    gradient = ysum[y]
    for d in (1, 7, 2, 6, 3, 5, 4):
        got(yr.at[d], yss.at[d], ysr.at[d])
        gradient = gradient + yr[d].astype(F32)

    new_first = BETA_ONE * m1[...] + (1.0 - BETA_ONE) * gradient
    new_second = BETA_TWO * m2[...] + (1.0 - BETA_TWO) * gradient * gradient
    first_fix = 1.0 - BETA_ONE**STEP
    second_fix = 1.0 - BETA_TWO**STEP
    direction = new_first / first_fix / (jnp.sqrt(new_second / second_fix) + EPSILON)
    dirb[dp] = direction.astype(BF16)
    for d in (4, 3, 5, 2, 6, 1, 7):
        put(dirb.at[dp], dirb.at[dp], ds_.at[d], dr_.at[d], py(d))
    put(dirb.at[dp], dirb.at[dp], dcs.at[0], dcr.at[0], py(0, True))
    n1[...] = new_first
    n2[...] = new_second
    for d in range(NY):
        for e in range(2):
            if d or e:
                peer = lax.rem(y - d + NY, NY) * 2 + (o if e else c)
                got(pu3.at[:, peer], u3s.at[d, e], u3r.at[d, e])
    for d in (1, 7, 2, 6, 3, 5, 4):
        slot = lax.rem(y - d + NY, NY) * 2 + c
        got(dirb.at[slot], ds_.at[d], dr_.at[d])
        put(dirb.at[slot], dirb.at[slot], dcs.at[d], dcr.at[d], py(0, True))
    for d in (0, 1, 7, 2, 6, 3, 5, 4):
        slot = lax.rem(y - d + NY, NY) * 2 + o
        got(dirb.at[slot], dcs.at[d], dcr.at[d])
    update = jnp.dot(
        pu3[...].reshape(RANK, RANK), dirb[...].reshape(RANK, WIDTH), preferred_element_type=F32
    )
    nw[...] = (wgt[...].astype(F32) - RATE * update).astype(BF16)
    for cp in sent:
        cp.wait_send()


def shards(tokens, cotangent, projection, weight, first_moment, second_moment):
    vmem = pl.BlockSpec(memory_space=pltpu.VMEM)
    hbm = pl.BlockSpec(memory_space=pl.ANY)
    dma = pltpu.SemaphoreType.DMA
    v = pltpu.VMEM
    scratch = [
        v((NX, RANK, WIDTH), BF16),
        v((NX, QUARTER, WIDTH), BF16),
        v((NX, QUARTER, WIDTH), BF16),
        v((CHUNKS, NZ, RANK // NZ, TC), BF16),
        v((CHUNKS, NZ, RANK // NZ, TC), BF16),
        v((CHUNKS, NZ, RANK // NZ, TC), BF16),
        v((NX, NY, 2, 32, WIDTH), F32),
        v((NX, NY, 32, WIDTH), BF16),
        v((NX, NY, 32, WIDTH), BF16),
        v((NX, NY, 32, WIDTH), BF16),
        v((NX, NY, 32, WIDTH), BF16),
        v((NY, 32, WIDTH), F32),
        v((NY, 32, WIDTH), BF16),
        v((NY, 32, WIDTH), BF16),
        v((2 * NY, 32, WIDTH), BF16),
        v((NX, 16, RANK), BF16),
        v((NZ, NX, 16, RANK), BF16),
        v((2, 16, 16, RANK), BF16),
        dma((2,)),
        dma((NX,)), dma((NX,)), dma((NX,)), dma((NX,)),
        dma((CHUNKS, NX)), dma((CHUNKS, NX)), dma((CHUNKS, NX)), dma((CHUNKS, NX)),
        dma((CHUNKS, NZ)), dma((CHUNKS, NZ)), dma((CHUNKS, NZ)), dma((CHUNKS, NZ)),
        dma((NX,)), dma((NX,)), dma((NX,)), dma((NX,)),
        dma((NY,)), dma((NY,)), dma((NY,)), dma((NY,)), dma((NY,)), dma((NY,)),
        dma((NX,)), dma((NX,)), dma((NZ,)), dma((NZ,)), dma((NY, 2)), dma((NY, 2)),
    ]
    return pl.pallas_call(
        kernel,
        out_shape=(
            jax.ShapeDtypeStruct(weight.shape, weight.dtype),
            jax.ShapeDtypeStruct(first_moment.shape, F32),
            jax.ShapeDtypeStruct(second_moment.shape, F32),
        ),
        in_specs=[hbm, hbm, vmem, vmem, vmem, vmem],
        out_specs=(vmem, vmem, vmem),
        scratch_shapes=scratch,
        compiler_params=pltpu.CompilerParams(
            collective_id=0, has_side_effects=True, vmem_limit_bytes=48 * 2**20
        ),
        cost_estimate=pl.CostEstimate(flops=1_800_000_000, bytes_accessed=4_500_000, transcendentals=8192),
    )(tokens, cotangent, projection, weight, first_moment, second_moment)


def solution(mesh):
    return jax.shard_map(
        shards,
        mesh=mesh,
        in_specs=(
            P("dp", "fsdp"),
            P("dp", "fsdp"),
            P("fsdp", None),
            P("dp", "fsdp"),
            P("dp", "fsdp"),
            P("dp", "fsdp"),
        ),
        out_specs=(P("dp", "fsdp"), P("dp", "fsdp"), P("dp", "fsdp")),
        check_vma=False,
    )
```

time: 362 us -> 106 us (0.29)
  waiting for transfers between devices: 318 us -> 0 us
  Pallas kernels: 0 us -> 97 us
  blocking collectives: 17 us -> 0 us
  between operations: 13.8 us -> 0.65 us
  matrix products: 9.27 us -> 0 us
  local copies, waits for them, and re-layouts: 1.38 us -> 8.16 us
    psum x1 -> x0, waiting for transfers between devices: 171 us -> none  [shards(): reduced = lax.psum(partial_low.astype(jnp.bfloat16), 'fsdp')]
    pallas_call x0 -> x1, Pallas kernels: none -> 97 us  [shards(): pl.pallas_call(kernel, out_shape=(jax.ShapeDtypeStruct(weight.shape, weig...]
    all_gather x1 -> x0, waiting for transfers between devices: 89.6 us -> none  [shards(): gathered = lax.all_gather(projection, 'fsdp', axis=0, tiled=True)]
    reduce_scatter x1 -> x0, waiting for transfers between devices: 56.5 us -> none  [shards(): lax.psum_scatter(lax.dot_general(reduced, cotangent, (((0,), (0,)), ((),...]
    all_gather x1 -> x0, blocking collectives: 17 us -> none  [shards(): full_direction = lax.all_gather(direction, 'dp', axis=0, tiled=True)]
    dot_general x3 -> x0, matrix products: 9.27 us -> none  [the longest x1 3.62 us: shards(): lax.dot_general(reduced, cotangent, (((0,), (0,)), ((), ())), preferred_e...]
    unnamed x10 -> x15, local copies, waits for them, and re-layouts: 1.38 us -> 8.16 us
  transfers between devices with their start and end apart: 3 -> 0, of which waited for: 3 -> 0; matrix products, arithmetic and copies ran while one was open for 0% -> 0% of each run, Pallas kernels for 0% -> 0%
where the time goes in v1:
time: 106 us
  Pallas kernels  97 us (92%)
  local copies, waits for them, and re-layouts  8.16 us (8%)
    pallas_call x1, Pallas kernels, shards(): pl.pallas_call(kernel, out_shape=(jax.ShapeDtypeStruct(weight.shape, weig...  97 us
    unnamed x15, local copies, waits for them, and re-layouts  8.16 us

profile of v1, /device:TPU:1, one launch (start us, length us, event | category | flops | bytes accessed | tf_op | source)
XLA Modules:
  0.0 105.8 jit_solution(12894034685516135267)
XLA Ops:
  0.6 0.0 copy-start
  0.6 1.4 %copy-done = bf16[3072,256]{1,0:T(8,128)(2,1)S(1)} copy-done((bf16[3072,256]{1,0:T(8,128)(2,1)S(1)}, bf16[3072,256]{1,0:T(8,128)(2,1)}, u32[]{:S(2)}) %copy-start) | copy-done | bytes 1572888
  2.0 0.0 copy-start.1
  2.0 1.4 %copy-done.1 = bf16[3072,256]{1,0:T(8,128)(2,1)S(1)} copy-done((bf16[3072,256]{1,0:T(8,128)(2,1)S(1)}, bf16[3072,256]{1,0:T(8,128)(2,1)}, u32[]{:S(2)}) %copy-start.1) | copy-done | bytes 1572888
  3.4 0.0 copy-start.2
  3.5 0.9 copy-done.2
  4.4 0.0 copy-start.3
  4.4 0.9 copy-done.3
  5.4 0.0 copy-start.4
  5.4 0.8 copy-done.4
  6.1 0.0 copy-start.5
  6.1 0.8 copy-done.5
  6.9 97.0 %shard_map.85 = (bf16[512,256]{1,0:T(8,128)(2,1)S(1)}, f32[32,256]{1,0:T(8,128)S(1)}, f32[32,256]{1,0:T(8,128)S(1)}) custom-call(bf16[3072,256]{1,0:T(8,128)(2,1)S(1)} %copy-done, bf16[3072,256]{1,0:T(8,128)(2,1)S(1)} %copy-done.1, bf16[256,512]{1,0:T(8,128)(2,1)S(1)} %copy-done.2, bf16[512,256]{1,0:T(8,128)(2,1)S(1)} %copy-done.3, f32[32,256]{1,0:T(8,128)S(1)} %copy-done.4, ...), custom_call_target="tpu_custom_call" | custom-call | flops 1800000000 | bytes 4500000 | tf_op jit(solution)/shard_map/pallas_call | solution.py:249
  103.8 0.7 copy.12
  104.5 0.6 copy.13
  105.2 0.6 copy.14
Async XLA Ops:
  0.6 1.4 %copy-start = (bf16[3072,256]{1,0:T(8,128)(2,1)S(1)}, bf16[3072,256]{1,0:T(8,128)(2,1)}, u32[]{:S(2)}) copy-start(bf16[3072,256]{1,0:T(8,128)(2,1)} %tok.1) | copy-start | bytes 4718596
  2.0 1.4 %copy-start.1 = (bf16[3072,256]{1,0:T(8,128)(2,1)S(1)}, bf16[3072,256]{1,0:T(8,128)(2,1)}, u32[]{:S(2)}) copy-start(bf16[3072,256]{1,0:T(8,128)(2,1)} %cot.1) | copy-start | bytes 4718596
  3.4 0.9 copy-start.2
  4.4 0.9 copy-start.3
  5.4 0.8 copy-start.4
  6.1 0.8 copy-start.5

commit v2 on v1

v2 whole, which is shorter than its diff:
```python
import functools

import jax
import jax.numpy as jnp
from jax import lax
from jax.experimental import pallas as pl
from jax.experimental.pallas import tpu as pltpu
from jax.sharding import PartitionSpec as P

STEP = 10
BETA_ONE = 0.9
BETA_TWO = 0.999
EPSILON = 1e-08
RATE = 0.1

NX, NY, NZ = 4, 8, 8
RANK = 512
WIDTH = 256
QUARTER = 768
SIZES = (256, 256, 256)
CHUNKS = len(SIZES)
STARTS = tuple(sum(SIZES[:k]) for k in range(CHUNKS))
MESH = pl.DeviceIdType.MESH
F32 = jnp.float32
BF16 = jnp.bfloat16


def kernel(
    tok, cot, proj_hbm, wgt_hbm, m1_hbm, m2_hbm, nw, n1, n2,
    proj, wgt, m1, m2, pt, t4, c4, psend, zr, zq, ag, acc, gs, gc, xs, xr, ysum, ys, yr, dirb,
    pu1, pu2, pu3, lsem, s_pt, s_py, s_pc, s_t, s_c, s_z, s_a, s_g, s_x, s_y, s_d, s_dc, s_u1, s_u2, s_u3,
):
    dp = lax.axis_index("dp")
    fs = lax.axis_index("fsdp")
    y, c = dp // 2, lax.rem(dp, 2)
    x, z = fs // NZ, lax.rem(fs, NZ)
    o = 1 - c

    def px(d):
        return (dp, lax.rem(x + d + NX, NX) * NZ + z)

    def pz(d):
        return (dp, x * NZ + lax.rem(z + d + NZ, NZ))

    def py(d, other=False):
        return (lax.rem(y + d + NY, NY) * 2 + (o if other else c), fs)

    sent = []

    def put(src, dst, sems, at, dev):
        cp = pltpu.make_async_remote_copy(
            src_ref=src, dst_ref=dst, send_sem=sems[0].at[at], recv_sem=sems[1].at[at], device_id=dev, device_id_type=MESH
        )
        cp.start()
        sent.append(cp)

    def got(dst, sems, at):
        pltpu.make_async_remote_copy(
            src_ref=dst, dst_ref=dst, send_sem=sems[0].at[at], recv_sem=sems[1].at[at], device_id=(dp, fs), device_id_type=MESH
        ).wait_recv()

    own_t = pltpu.make_async_copy(tok.at[pl.ds(x * QUARTER, QUARTER)], t4.at[0], lsem.at[0])
    own_c = pltpu.make_async_copy(cot.at[pl.ds(x * QUARTER, QUARTER)], c4.at[0], lsem.at[1])
    loads = [
        pltpu.make_async_copy(src, dst, lsem.at[i + 2])
        for i, (src, dst) in enumerate(((proj_hbm, proj), (wgt_hbm, wgt), (m1_hbm, m1), (m2_hbm, m2)))
    ]
    for load in loads:
        load.start()
    own_t.start()
    own_c.start()

    barrier = pltpu.get_barrier_semaphore()
    for d in range(1, NX):
        pl.semaphore_signal(barrier, inc=1, device_id=px(d), device_id_type=MESH)
    for d in range(1, NZ):
        pl.semaphore_signal(barrier, inc=1, device_id=pz(d), device_id_type=MESH)
    for d in range(NY):
        pl.semaphore_signal(barrier, inc=1, device_id=py(d, True), device_id_type=MESH)
        if d:
            pl.semaphore_signal(barrier, inc=1, device_id=py(d), device_id_type=MESH)
    loads[0].wait()
    pt[0] = proj[...].T
    pu1[x] = proj[pl.ds(dp * 16, 16)]
    pl.semaphore_wait(barrier, NX - 1 + NZ - 1 + 2 * NY - 1)

    def ranks(core, row):
        return pl.ds(core * 256 + lax.rem(row + NY, 4) * 64, 64)

    others = pl.ds(1, NX - 1)
    for d in (2, 1, 3):
        put(pt.at[0, ranks(c, y)], pt.at[d, ranks(c, y)], s_pt, (d,), px(d))
    for d in (2, 1, 3):
        put(pu1.at[x], pu1.at[x], s_u1, (d,), px(d))
    for k in range(CHUNKS):
        for d in (2, 1, 3):
            rows = pl.ds(lax.rem(x + d, NX) * QUARTER + STARTS[k], SIZES[k])
            put(tok.at[rows], t4.at[d, pl.ds(STARTS[k], SIZES[k])], s_t, (k, d), px(d))

    for d in (1, 3, 2):
        got(pt.at[d, ranks(c, y)], s_pt, (d,))
    far = 2 - 4 * c
    for i, d in enumerate((1, -1, far)):
        put(pt.at[others, ranks(c, y)], pt.at[others, ranks(c, y)], s_py, (i,), py(d))
    put(pt.at[others, ranks(c, y)], pt.at[others, ranks(c, y)], s_pc, (3,), py(0, True))

    for d in (1, 3, 2):
        got(pu1.at[lax.rem(x - d + NX, NX)], s_u1, (d,))
    pu2[z] = pu1[...]

    def relay(step):
        up, down = lax.rem(z - step + 1 + NZ, NZ), lax.rem(z + step - 1, NZ)
        if step > 1:
            got(pu2.at[up], s_u2, (step - 2,))
            got(pu2.at[down], s_u2, (step + 2,))
        put(pu2.at[up], pu2.at[up], s_u2, (step - 1,), pz(1))
        if step < 4:
            put(pu2.at[down], pu2.at[down], s_u2, (step + 3,), pz(-1))

    relay(1)
    for i, d in enumerate((1, -1, far)):
        got(pt.at[others, ranks(c, y - d)], s_py, (i,))
        put(pt.at[others, ranks(c, y - d)], pt.at[others, ranks(c, y - d)], s_pc, (i,), py(0, True))
    relay(2)
    for i, d in enumerate((1, -1, -far, 0)):
        got(pt.at[others, ranks(o, y - d)], s_pc, (i,))
    own_t.wait()

    def send_cot():
        for k in range(CHUNKS):
            for d in (2, 1, 3):
                rows = pl.ds(lax.rem(x + d, NX) * QUARTER + STARTS[k], SIZES[k])
                put(cot.at[rows], c4.at[d, pl.ds(STARTS[k], SIZES[k])], s_c, (k, d), px(d))

    def at(d):
        return lax.rem(z + d + NZ, NZ)

    def sign(k):
        return 1 if k % 2 == 0 else -1

    def partial(k):
        rows = pl.ds(STARTS[k], SIZES[k])
        for d in (1, 3, 2):
            got(t4.at[d, rows], s_t, (k, d))
        low = None
        for d in range(NX):
            part = lax.dot_general(
                pt[d], t4[d, rows], (((1,), (1,)), ((), ())), preferred_element_type=F32
            )
            low = part if low is None else low + part
        psend[k][...] = low.astype(BF16).reshape(NZ, RANK // NZ, SIZES[k])
        e = sign(k)
        for owner, to, slot in ((-4, -e, 0), (-2 * e, e, 1), (e, -e, 2), (3 * e, e, 3), (-e, -e, 5)):
            put(psend[k].at[at(owner)], zr[k].at[slot], s_z, (k, slot), pz(to))

    def middle(k):
        e = sign(k)
        for owner, one, two, slot in ((-3 * e, 0, 1, 6), (2 * e, 2, 3, 7)):
            got(zr[k].at[one], s_z, (k, one))
            got(zr[k].at[two], s_z, (k, two))
            both = zr[k][one].astype(F32) + zr[k][two].astype(F32)
            zq[k][slot - 6] = (psend[k][at(owner)].astype(F32) + both).astype(BF16)
            put(zq[k].at[slot - 6], zr[k].at[slot], s_z, (k, slot), pz(owner))

    def reduce(k):
        e = sign(k)
        total = psend[k][z].astype(F32)
        for slot in (5, 7, 6):
            got(zr[k].at[slot], s_z, (k, slot))
            total = total + zr[k][slot].astype(F32)
        ag[k][z] = total.astype(BF16)
        for d in (3 * e, -2 * e, e):
            put(ag[k].at[z], ag[k].at[z], s_a, (k, d % 8), pz(d))

    def arrived(k, d):
        got(ag[k].at[at(-d)], s_a, (k, d % 8))

    def forward(k):
        e = sign(k)
        for d in (-2 * e, 3 * e):
            arrived(k, d)
            for f in (e, -e):
                put(ag[k].at[at(-d)], ag[k].at[at(-d)], s_a, (k, (d + f) % 8), pz(f))

    def send_update_rows():
        got(pu2.at[lax.rem(z - 4 + NZ, NZ)], s_u2, (3,))
        for d in range(NY):
            for e in range(2):
                peer = lax.rem(y + d, NY) * 2 + (o if e else c)
                src = pu2.at[pl.ds(2 * lax.rem(peer, 4), 2), peer // 4]
                if d == 0 and e == 0:
                    pu3[:, dp] = pu2[pl.ds(2 * lax.rem(peer, 4), 2), peer // 4]
                else:
                    put(src, pu3.at[:, dp], s_u3, (d, e), py(d, e == 1))

    for k in range(CHUNKS + 3):
        if k < CHUNKS:
            partial(k)
        if k == CHUNKS - 2:
            send_cot()
        if 0 <= k - 1 < CHUNKS:
            middle(k - 1)
        if 0 <= k - 2 < CHUNKS:
            reduce(k - 2)
        if 0 <= k - 3 < CHUNKS:
            forward(k - 3)
        if k < 2:
            relay(k + 3)
        if k == 2:
            send_update_rows()

    own_c.wait()
    for k in range(CHUNKS):
        rows = pl.ds(STARTS[k], SIZES[k])
        e = sign(k)
        for d in (e, -e, 2 * e, -3 * e, 4):
            arrived(k, d)
        low = ag[k][...].reshape(RANK, SIZES[k])
        for d in (0, 1, 3, 2):
            if d:
                got(c4.at[d, rows], s_c, (k, d))
            part = jnp.dot(low, c4[d, rows], preferred_element_type=F32).reshape(NY, 2, 32, WIDTH)
            acc[d] = part if k == 0 else acc[d] + part

    halves = (0, 1)
    for h in halves:
        for d in (2, 1, 3, 0):
            gs[h, d] = acc[d, :, o, h * 16 : h * 16 + 16].astype(BF16)
            put(gs.at[h, d], gc.at[h, d], s_g, (h, d), py(0, True))

    def paired(h, d):
        got(gc.at[h, d], s_g, (h, d))
        return acc[d, :, c, h * 16 : h * 16 + 16] + gc[h, d].astype(F32)

    for h in halves:
        for d in (2, 1, 3):
            xs[h, d] = paired(h, d).astype(BF16)
            put(xs.at[h, d], xr.at[h, d], s_x, (h, d), px(-d))
    for h in halves:
        total = paired(h, 0)
        for d in (1, 3, 2):
            got(xr.at[h, d], s_x, (h, d))
            total = total + xr[h, d].astype(F32)
        ysum[h] = total
        ys[h] = total.astype(BF16)
        for d in (4, 3, 5, 2, 6, 1, 7):
            put(ys.at[h, lax.rem(y + d, NY)], yr.at[h, d], s_y, (h, d), py(d))
    for load in loads[1:]:
        load.wait()
    first_fix = 1.0 - BETA_ONE**STEP
    second_fix = 1.0 - BETA_TWO**STEP
    for h in halves:
        gradient = ysum[h, y]
        for d in (1, 7, 2, 6, 3, 5, 4):
            got(yr.at[h, d], s_y, (h, d))
            gradient = gradient + yr[h, d].astype(F32)
        rows = pl.ds(h * 16, 16)
        new_first = BETA_ONE * m1[rows] + (1.0 - BETA_ONE) * gradient
        new_second = BETA_TWO * m2[rows] + (1.0 - BETA_TWO) * gradient * gradient
        direction = new_first / first_fix / (jnp.sqrt(new_second / second_fix) + EPSILON)
        dirb[y, c, h] = direction.astype(BF16)
        for d in (4, 3, 5, 2, 6, 1, 7):
            put(dirb.at[y, c, h], dirb.at[y, c, h], s_d, (h, d), py(d))
        n1[rows] = new_first
        n2[rows] = new_second
    for d in range(NY):
        for e in range(2):
            if d or e:
                peer = lax.rem(y - d + NY, NY) * 2 + (o if e else c)
                got(pu3.at[:, peer], s_u3, (d, e))
    for h in halves:
        for d in (1, 7, 2, 6, 3, 5, 4):
            got(dirb.at[lax.rem(y - d + NY, NY), c, h], s_d, (h, d))
        put(dirb.at[:, c, h], dirb.at[:, c, h], s_dc, (h,), py(0, True))
    for h in halves:
        got(dirb.at[:, o, h], s_dc, (h,))
    update = jnp.dot(
        pu3[...].reshape(RANK, RANK), dirb[...].reshape(RANK, WIDTH), preferred_element_type=F32
    )
    nw[...] = (wgt[...].astype(F32) - RATE * update).astype(BF16)
    for cp in sent:
        cp.wait_send()


def hand_over(nw, n1, n2, nw_out, n1_out, n2_out, a, b, e, sems):
    trips = ((nw, a, nw_out), (n1, b, n1_out), (n2, e, n2_out))
    ins = [pltpu.make_async_copy(src, mid, sems.at[0, i]) for i, (src, mid, _) in enumerate(trips)]
    outs = [pltpu.make_async_copy(mid, dst, sems.at[1, i]) for i, (_, mid, dst) in enumerate(trips)]
    for copy in ins:
        copy.start()
    for first, second in zip(ins, outs):
        first.wait()
        second.start()
    for copy in outs:
        copy.wait()


def shards(tokens, cotangent, projection, weight, first_moment, second_moment):
    vmem = pl.BlockSpec(memory_space=pltpu.VMEM)
    hbm = pl.BlockSpec(memory_space=pltpu.HBM)
    dma = pltpu.SemaphoreType.DMA
    v = pltpu.VMEM

    def pair(*n):
        return dma(n), dma(n)

    scratch = [
        v(projection.shape, BF16),
        v(weight.shape, BF16),
        v(first_moment.shape, F32),
        v(second_moment.shape, F32),
        v((NX, RANK, WIDTH), BF16),
        v((NX, QUARTER, WIDTH), BF16),
        v((NX, QUARTER, WIDTH), BF16),
        tuple(v((NZ, RANK // NZ, n), BF16) for n in SIZES),
        tuple(v((NZ, RANK // NZ, n), BF16) for n in SIZES),
        tuple(v((2, RANK // NZ, n), BF16) for n in SIZES),
        tuple(v((NZ, RANK // NZ, n), BF16) for n in SIZES),
        v((NX, NY, 2, 32, WIDTH), F32),
        v((2, NX, NY, 16, WIDTH), BF16),
        v((2, NX, NY, 16, WIDTH), BF16),
        v((2, NX, NY, 16, WIDTH), BF16),
        v((2, NX, NY, 16, WIDTH), BF16),
        v((2, NY, 16, WIDTH), F32),
        v((2, NY, 16, WIDTH), BF16),
        v((2, NY, 16, WIDTH), BF16),
        v((NY, 2, 2, 16, WIDTH), BF16),
        v((NX, 16, RANK), BF16),
        v((NZ, NX, 16, RANK), BF16),
        v((2, 16, 16, RANK), BF16),
        dma((6,)),
        pair(NX), pair(3), pair(4),
        pair(CHUNKS, NX), pair(CHUNKS, NX), pair(CHUNKS, NZ), pair(CHUNKS, NZ),
        pair(2, NX), pair(2, NX), pair(2, NY), pair(2, NY), pair(2),
        pair(NX), pair(7), pair(NY, 2),
    ]
    shapes = (
        jax.ShapeDtypeStruct(weight.shape, weight.dtype),
        jax.ShapeDtypeStruct(first_moment.shape, F32),
        jax.ShapeDtypeStruct(second_moment.shape, F32),
    )
    results = pl.pallas_call(
        kernel,
        out_shape=shapes,
        in_specs=[hbm] * 6,
        out_specs=(vmem, vmem, vmem),
        scratch_shapes=scratch,
        compiler_params=pltpu.CompilerParams(
            collective_id=0, has_side_effects=True, vmem_limit_bytes=63 * 2**20
        ),
        cost_estimate=pl.CostEstimate(flops=1_800_000_000, bytes_accessed=4_500_000, transcendentals=8192),
    )(tokens, cotangent, projection, weight, first_moment, second_moment)
    return pl.pallas_call(
        hand_over,
        out_shape=shapes,
        in_specs=[hbm] * 3,
        out_specs=(hbm, hbm, hbm),
        scratch_shapes=[v(t.shape, t.dtype) for t in shapes] + [dma((2, 3))],
        compiler_params=pltpu.CompilerParams(vmem_limit_bytes=63 * 2**20),
    )(*results)


def solution(mesh):
    return jax.shard_map(
        shards,
        mesh=mesh,
        in_specs=(
            P("dp", "fsdp"),
            P("dp", "fsdp"),
            P("fsdp", None),
            P("dp", "fsdp"),
            P("dp", "fsdp"),
            P("dp", "fsdp"),
        ),
        out_specs=(P("dp", "fsdp"), P("dp", "fsdp"), P("dp", "fsdp")),
        check_vma=False,
    )
```

time: 106 us -> 85.4 us (0.81)
  Pallas kernels: 97 us -> 84.6 us
  local copies, waits for them, and re-layouts: 8.16 us -> 0 us
    pallas_call x1 -> x2, Pallas kernels: 97 us -> 84.6 us  [the longest x1 82.9 us: shards(): pl.pallas_call(kernel, out_shape=shapes, in_specs=[hbm] * 6, out_specs=(v...]
    unnamed x15 -> x0, local copies, waits for them, and re-layouts: 8.16 us -> none
where the time goes in v2:
time: 85.4 us; the launch traced here: 85.3 us
  Pallas kernels  84.6 us (99%)
    pallas_call x1, Pallas kernels, shards(): pl.pallas_call(kernel, out_shape=shapes, in_specs=[hbm] * 6, out_specs=(v...  82.9 us
    pallas_call x1, Pallas kernels, shards(): pl.pallas_call(hand_over, out_shape=shapes, in_specs=[hbm] * 3, out_specs...  1.71 us

profile of v2, /device:TPU:1, one launch (start us, length us, event | category | flops | bytes accessed | tf_op | source)
XLA Modules:
  0.0 85.3 jit_solution(4033228514649353522)
XLA Ops:
  0.6 82.9 %shard_map.85 = (bf16[512,256]{1,0:T(8,128)(2,1)}, f32[32,256]{1,0:T(8,128)}, f32[32,256]{1,0:T(8,128)}) custom-call(bf16[3072,256]{1,0:T(8,128)(2,1)} %tok.1, bf16[3072,256]{1,0:T(8,128)(2,1)} %cot.1, bf16[256,512]{1,0:T(8,128)(2,1)} %proj_hbm.1, bf16[512,256]{1,0:T(8,128)(2,1)} %wgt_hbm.1, f32[32,256]{1,0:T(8,128)} %m1_hbm.1, f32[32,256]{1,0:T(8,128)} %m2_hbm.1), custom_call_target="tpu_custom_call" | custom-call | flops 1800000000 | bytes 4500000 | tf_op jit(solution)/shard_map/pallas_call | solution.py:342
  83.6 1.7 %shard_map.86 = (bf16[512,256]{1,0:T(8,128)(2,1)}, f32[32,256]{1,0:T(8,128)}, f32[32,256]{1,0:T(8,128)}) custom-call(bf16[512,256]{1,0:T(8,128)(2,1)} %get-tuple-element.6.nw, f32[32,256]{1,0:T(8,128)} %get-tuple-element.7.n1, f32[32,256]{1,0:T(8,128)} %get-tuple-element.8.n2), custom_call_target="tpu_custom_call" | custom-call | tf_op jit(solution)/shard_map/pallas_call | solution.py:353

commit v3 on v2

v3 whole, which is shorter than its diff:
```python
import functools

import jax
import jax.numpy as jnp
from jax import lax
from jax.experimental import pallas as pl
from jax.experimental.pallas import tpu as pltpu
from jax.sharding import PartitionSpec as P

STEP = 10
BETA_ONE = 0.9
BETA_TWO = 0.999
EPSILON = 1e-08
RATE = 0.1

NX, NY, NZ = 4, 8, 8
RANK = 512
WIDTH = 256
QUARTER = 768
SIZES = (256, 256, 256)
CHUNKS = len(SIZES)
STARTS = tuple(sum(SIZES[:k]) for k in range(CHUNKS))
MESH = pl.DeviceIdType.MESH
F32 = jnp.float32
BF16 = jnp.bfloat16


def kernel(
    tok, cot, proj_hbm, wgt_hbm, m1_hbm, m2_hbm, nw, n1, n2,
    proj, wgt, m1, m2, pt, t4, c4, psend, zr, zq, ag, acc, gs, gc, xs, xr, ysum, ys, yr, dirb,
    pu1, pu2, pu3, y2sum, y2s, y2r, x2s, x2r,
    lsem, s_out, s_pt, s_py, s_pc, s_t, s_c, s_z, s_a, s_g, s_x, s_y, s_y2, s_x2, s_d, s_dc, s_u1, s_u2, s_u3,
):
    dp = lax.axis_index("dp")
    fs = lax.axis_index("fsdp")
    y, c = dp // 2, lax.rem(dp, 2)
    x, z = fs // NZ, lax.rem(fs, NZ)
    o = 1 - c

    def px(d):
        return (dp, lax.rem(x + d + NX, NX) * NZ + z)

    def pz(d):
        return (dp, x * NZ + lax.rem(z + d + NZ, NZ))

    def py(d, other=False):
        return (lax.rem(y + d + NY, NY) * 2 + (o if other else c), fs)

    sent = []

    def put(src, dst, sem, dev):
        cp = pltpu.make_async_remote_copy(
            src_ref=src, dst_ref=dst, send_sem=s_out, recv_sem=sem, device_id=dev, device_id_type=MESH
        )
        cp.start()
        sent.append(cp)

    def got(dst, sem):
        pltpu.make_async_remote_copy(
            src_ref=dst, dst_ref=dst, send_sem=s_out, recv_sem=sem, device_id=(dp, fs), device_id_type=MESH
        ).wait_recv()

    own_t = pltpu.make_async_copy(tok.at[pl.ds(x * QUARTER, QUARTER)], t4.at[0], lsem.at[0])
    own_c = pltpu.make_async_copy(cot.at[pl.ds(x * QUARTER, QUARTER)], c4.at[0], lsem.at[1])
    loads = [
        pltpu.make_async_copy(src, dst, lsem.at[i + 2])
        for i, (src, dst) in enumerate(((proj_hbm, proj), (wgt_hbm, wgt), (m1_hbm, m1), (m2_hbm, m2)))
    ]
    for load in loads:
        load.start()
    own_t.start()
    own_c.start()

    barrier = pltpu.get_barrier_semaphore()
    for d in range(1, NX):
        pl.semaphore_signal(barrier, inc=1, device_id=px(d), device_id_type=MESH)
    for d in range(1, NZ):
        pl.semaphore_signal(barrier, inc=1, device_id=pz(d), device_id_type=MESH)
    for d in range(NY):
        pl.semaphore_signal(barrier, inc=1, device_id=py(d, True), device_id_type=MESH)
        if d:
            pl.semaphore_signal(barrier, inc=1, device_id=py(d), device_id_type=MESH)
    loads[0].wait()
    pt[0] = proj[...].T
    pu1[x] = proj[pl.ds(dp * 16, 16)]
    pl.semaphore_wait(barrier, NX - 1 + NZ - 1 + 2 * NY - 1)

    def ranks(core, row):
        return pl.ds(core * 256 + lax.rem(row + NY, 4) * 64, 64)

    others = pl.ds(1, NX - 1)
    for d in (2, 1, 3):
        put(pt.at[0, ranks(c, y)], pt.at[d, ranks(c, y)], s_pt.at[0], px(d))
    for d in (2, 1, 3):
        put(pu1.at[x], pu1.at[x], s_u1.at[0], px(d))
    for k in range(CHUNKS):
        for d in (2, 1, 3):
            rows = pl.ds(lax.rem(x + d, NX) * QUARTER + STARTS[k], SIZES[k])
            put(tok.at[rows], t4.at[d, pl.ds(STARTS[k], SIZES[k])], s_t.at[k], px(d))

    got(pt.at[others, ranks(c, y)], s_pt.at[0])
    far = 2 - 4 * c
    for i, d in enumerate((1, -1, far)):
        put(pt.at[others, ranks(c, y)], pt.at[others, ranks(c, y)], s_py.at[i], py(d))
    put(pt.at[others, ranks(c, y)], pt.at[others, ranks(c, y)], s_pc.at[0], py(0, True))

    got(pu1.at[others], s_u1.at[0])
    pu2[z] = pu1[...]

    def relay(step):
        up, down = lax.rem(z - step + 1 + NZ, NZ), lax.rem(z + step - 1, NZ)
        if step > 1:
            got(pu2.at[up], s_u2.at[step - 2])
            got(pu2.at[down], s_u2.at[step + 2])
        put(pu2.at[up], pu2.at[up], s_u2.at[step - 1], pz(1))
        if step < 4:
            put(pu2.at[down], pu2.at[down], s_u2.at[step + 3], pz(-1))

    relay(1)
    for i, d in enumerate((1, -1, far)):
        got(pt.at[others, ranks(c, y - d)], s_py.at[i])
        put(pt.at[others, ranks(c, y - d)], pt.at[others, ranks(c, y - d)], s_pc.at[0], py(0, True))
    relay(2)
    got(pt.at[others, pl.ds(o * 256, 256)], s_pc.at[0])
    own_t.wait()

    def send_cot():
        for k in range(CHUNKS):
            for d in (2, 1, 3):
                rows = pl.ds(lax.rem(x + d, NX) * QUARTER + STARTS[k], SIZES[k])
                put(cot.at[rows], c4.at[d, pl.ds(STARTS[k], SIZES[k])], s_c.at[k], px(d))

    def at(d):
        return lax.rem(z + d + NZ, NZ)

    def sign(k):
        return 1 if k % 2 == 0 else -1

    def partial(k):
        rows = pl.ds(STARTS[k], SIZES[k])
        got(t4.at[others, rows], s_t.at[k])
        low = None
        for d in range(NX):
            part = lax.dot_general(
                pt[d], t4[d, rows], (((1,), (1,)), ((), ())), preferred_element_type=F32
            )
            low = part if low is None else low + part
        psend[k][...] = low.astype(BF16).reshape(NZ, RANK // NZ, SIZES[k])
        e = sign(k)
        for owner, to, slot in ((-4, -e, 0), (-2 * e, e, 1), (e, -e, 2), (3 * e, e, 3), (-e, -e, 4)):
            put(psend[k].at[at(owner)], zr[k].at[slot], s_z.at[k, slot // 4], pz(to))

    def middle(k):
        e = sign(k)
        got(zr[k].at[pl.ds(0, 4)], s_z.at[k, 0])
        for owner, one, two, slot in ((-3 * e, 0, 1, 5), (2 * e, 2, 3, 6)):
            both = zr[k][one].astype(F32) + zr[k][two].astype(F32)
            zq[k][slot - 5] = (psend[k][at(owner)].astype(F32) + both).astype(BF16)
            put(zq[k].at[slot - 5], zr[k].at[slot], s_z.at[k, 1], pz(owner))

    def reduce(k):
        e = sign(k)
        total = psend[k][z].astype(F32)
        got(zr[k].at[pl.ds(4, 3)], s_z.at[k, 1])
        for slot in (4, 5, 6):
            total = total + zr[k][slot].astype(F32)
        ag[k][z] = total.astype(BF16)
        for d in (3 * e, -2 * e, e):
            put(ag[k].at[z], ag[k].at[z], s_a.at[k, 1 if d == e else 0], pz(d))

    def forward(k):
        e = sign(k)
        got(ag[k].at[pl.ds(0, 2)], s_a.at[k, 0])
        for d in (-2 * e, 3 * e):
            for f in (e, -e):
                put(ag[k].at[at(-d)], ag[k].at[at(-d)], s_a.at[k, 1], pz(f))

    def send_update_rows():
        got(pu2.at[lax.rem(z - 4 + NZ, NZ)], s_u2.at[3])
        for d in range(NY):
            for e in range(2):
                peer = lax.rem(y + d, NY) * 2 + (o if e else c)
                src = pu2.at[pl.ds(2 * lax.rem(peer, 4), 2), peer // 4]
                if d == 0 and e == 0:
                    pu3[:, dp] = pu2[pl.ds(2 * lax.rem(peer, 4), 2), peer // 4]
                else:
                    put(src, pu3.at[:, dp], s_u3.at[0], py(d, e == 1))

    for k in range(CHUNKS + 3):
        if k < CHUNKS:
            partial(k)
        if k == CHUNKS - 2:
            send_cot()
        if 0 <= k - 1 < CHUNKS:
            middle(k - 1)
        if 0 <= k - 2 < CHUNKS:
            reduce(k - 2)
        if 0 <= k - 3 < CHUNKS:
            forward(k - 3)
        if k < 2:
            relay(k + 3)
        if k == 2:
            send_update_rows()

    own_c.wait()
    for k in range(CHUNKS):
        rows = pl.ds(STARTS[k], SIZES[k])
        got(ag[k].at[pl.ds(0, 5)], s_a.at[k, 1])
        got(c4.at[others, rows], s_c.at[k])
        low = ag[k][...].reshape(RANK, SIZES[k])
        for d in (2, 1, 3, 0):
            part = jnp.dot(low, c4[d, rows], preferred_element_type=F32).reshape(NY, 2, 32, WIDTH)
            acc[d] = part if k == 0 else acc[d] + part

    halves = (0, 1)
    order = (2, 1, 3, 0)
    groups = (pl.ds(0, 1), pl.ds(1, 2), pl.ds(3, 1))
    for h in halves:
        for i, group in enumerate(groups):
            for slot in range(group.start, group.start + group.size):
                gs[h, slot] = acc[order[slot], :, o, h * 16 : h * 16 + 16].astype(BF16)
            put(gs.at[h, group], gc.at[h, group], s_g.at[h, i], py(0, True))

    def paired(h, slot):
        return acc[order[slot], :, c, h * 16 : h * 16 + 16] + gc[h, slot].astype(F32)

    for h in halves:
        got(gc.at[h, groups[0]], s_g.at[h, 0])
        total = paired(h, 0)
        y2sum[h] = total
        y2s[h] = total.astype(BF16)
        for d in (4, 3, 5, 2, 6, 1, 7):
            put(y2s.at[h, lax.rem(y + d, NY)], y2r.at[h, d], s_y2.at[h], py(d))
        got(gc.at[h, groups[1]], s_g.at[h, 1])
        for slot in (1, 2):
            xs[h, slot - 1] = paired(h, slot).astype(BF16)
            put(xs.at[h, slot - 1], xr.at[h, slot - 1], s_x.at[h], px(-order[slot]))
    for h in halves:
        got(gc.at[h, groups[2]], s_g.at[h, 2])
        total = paired(h, 3)
        got(xr.at[h], s_x.at[h])
        total = total + xr[h, 0].astype(F32) + xr[h, 1].astype(F32)
        ysum[h] = total
        ys[h] = total.astype(BF16)
        for d in (4, 3, 5, 2, 6, 1, 7):
            put(ys.at[h, lax.rem(y + d, NY)], yr.at[h, d], s_y.at[h], py(d))
    for h in halves:
        got(y2r.at[h, pl.ds(1, NY - 1)], s_y2.at[h])
        total = y2sum[h, y]
        for d in range(1, NY):
            total = total + y2r[h, d].astype(F32)
        x2s[h] = total.astype(BF16)
        put(x2s.at[h], x2r.at[h], s_x2.at[h], px(2))
    for load in loads[1:]:
        load.wait()
    first_fix = 1.0 - BETA_ONE**STEP
    second_fix = 1.0 - BETA_TWO**STEP
    for h in halves:
        got(yr.at[h, pl.ds(1, NY - 1)], s_y.at[h])
        got(x2r.at[h], s_x2.at[h])
        gradient = ysum[h, y] + x2r[h].astype(F32)
        for d in range(1, NY):
            gradient = gradient + yr[h, d].astype(F32)
        rows = pl.ds(h * 16, 16)
        new_first = BETA_ONE * m1[rows] + (1.0 - BETA_ONE) * gradient
        new_second = BETA_TWO * m2[rows] + (1.0 - BETA_TWO) * gradient * gradient
        direction = new_first / first_fix / (jnp.sqrt(new_second / second_fix) + EPSILON)
        dirb[y, c, h] = direction.astype(BF16)
        for d in (4, 3, 5, 2, 6, 1, 7):
            put(dirb.at[y, c, h], dirb.at[y, c, h], s_d.at[h], py(d))
        n1[rows] = new_first
        n2[rows] = new_second
    got(pu3.at[:, pl.ds(0, 2 * NY - 1)], s_u3.at[0])
    for h in halves:
        got(dirb.at[pl.ds(0, NY - 1), c, h], s_d.at[h])
        put(dirb.at[:, c, h], dirb.at[:, c, h], s_dc.at[h], py(0, True))
    for h in halves:
        got(dirb.at[:, o, h], s_dc.at[h])
    update = jnp.dot(
        pu3[...].reshape(RANK, RANK), dirb[...].reshape(RANK, WIDTH), preferred_element_type=F32
    )
    nw[...] = (wgt[...].astype(F32) - RATE * update).astype(BF16)
    for cp in sent:
        cp.wait_send()


def hand_over(nw, n1, n2, nw_out, n1_out, n2_out, a, b, e, sems):
    trips = ((nw, a, nw_out), (n1, b, n1_out), (n2, e, n2_out))
    ins = [pltpu.make_async_copy(src, mid, sems.at[0, i]) for i, (src, mid, _) in enumerate(trips)]
    outs = [pltpu.make_async_copy(mid, dst, sems.at[1, i]) for i, (_, mid, dst) in enumerate(trips)]
    for copy in ins:
        copy.start()
    for first, second in zip(ins, outs):
        first.wait()
        second.start()
    for copy in outs:
        copy.wait()


def shards(tokens, cotangent, projection, weight, first_moment, second_moment):
    vmem = pl.BlockSpec(memory_space=pltpu.VMEM)
    hbm = pl.BlockSpec(memory_space=pltpu.HBM)
    dma = pltpu.SemaphoreType.DMA
    v = pltpu.VMEM
    scratch = [
        v(projection.shape, BF16),
        v(weight.shape, BF16),
        v(first_moment.shape, F32),
        v(second_moment.shape, F32),
        v((NX, RANK, WIDTH), BF16),
        v((NX, QUARTER, WIDTH), BF16),
        v((NX, QUARTER, WIDTH), BF16),
        tuple(v((NZ, RANK // NZ, n), BF16) for n in SIZES),
        tuple(v((NZ, RANK // NZ, n), BF16) for n in SIZES),
        tuple(v((2, RANK // NZ, n), BF16) for n in SIZES),
        tuple(v((NZ, RANK // NZ, n), BF16) for n in SIZES),
        v((NX, NY, 2, 32, WIDTH), F32),
        v((2, NX, NY, 16, WIDTH), BF16),
        v((2, NX, NY, 16, WIDTH), BF16),
        v((2, 2, NY, 16, WIDTH), BF16),
        v((2, 2, NY, 16, WIDTH), BF16),
        v((2, NY, 16, WIDTH), F32),
        v((2, NY, 16, WIDTH), BF16),
        v((2, NY, 16, WIDTH), BF16),
        v((NY, 2, 2, 16, WIDTH), BF16),
        v((NX, 16, RANK), BF16),
        v((NZ, NX, 16, RANK), BF16),
        v((2, 16, 16, RANK), BF16),
        v((2, NY, 16, WIDTH), F32),
        v((2, NY, 16, WIDTH), BF16),
        v((2, NY, 16, WIDTH), BF16),
        v((2, 16, WIDTH), BF16),
        v((2, 16, WIDTH), BF16),
        dma((6,)), dma(()),
        dma((1,)), dma((3,)), dma((1,)),
        dma((CHUNKS,)), dma((CHUNKS,)), dma((CHUNKS, 2)), dma((CHUNKS, 2)),
        dma((2, 3)), dma((2,)), dma((2,)), dma((2,)), dma((2,)), dma((2,)), dma((2,)),
        dma((1,)), dma((7,)), dma((1,)),
    ]
    shapes = (
        jax.ShapeDtypeStruct(weight.shape, weight.dtype),
        jax.ShapeDtypeStruct(first_moment.shape, F32),
        jax.ShapeDtypeStruct(second_moment.shape, F32),
    )
    results = pl.pallas_call(
        kernel,
        out_shape=shapes,
        in_specs=[hbm] * 6,
        out_specs=(vmem, vmem, vmem),
        scratch_shapes=scratch,
        compiler_params=pltpu.CompilerParams(
            collective_id=0, has_side_effects=True, vmem_limit_bytes=63 * 2**20
        ),
        cost_estimate=pl.CostEstimate(flops=1_800_000_000, bytes_accessed=4_500_000, transcendentals=8192),
    )(tokens, cotangent, projection, weight, first_moment, second_moment)
    return pl.pallas_call(
        hand_over,
        out_shape=shapes,
        in_specs=[hbm] * 3,
        out_specs=(hbm, hbm, hbm),
        scratch_shapes=[v(t.shape, t.dtype) for t in shapes] + [dma((2, 3))],
        compiler_params=pltpu.CompilerParams(vmem_limit_bytes=63 * 2**20),
    )(*results)


def solution(mesh):
    return jax.shard_map(
        shards,
        mesh=mesh,
        in_specs=(
            P("dp", "fsdp"),
            P("dp", "fsdp"),
            P("fsdp", None),
            P("dp", "fsdp"),
            P("dp", "fsdp"),
            P("dp", "fsdp"),
        ),
        out_specs=(P("dp", "fsdp"), P("dp", "fsdp"), P("dp", "fsdp")),
        check_vma=False,
    )
```

time: 85.4 us -> 80.4 us (0.941)
  Pallas kernels: 84.6 us -> 79.6 us
    pallas_call x1, Pallas kernels: 82.9 us -> 77.9 us  [shards(): pl.pallas_call(kernel, out_shape=shapes, in_specs=[hbm] * 6, out_specs=(v...]
where the time goes in v3:
time: 80.4 us; the launch traced here: 80.2 us
  Pallas kernels  79.6 us (99%)
    pallas_call x1, Pallas kernels, shards(): pl.pallas_call(kernel, out_shape=shapes, in_specs=[hbm] * 6, out_specs=(v...  77.9 us
    pallas_call x1, Pallas kernels, shards(): pl.pallas_call(hand_over, out_shape=shapes, in_specs=[hbm] * 3, out_specs...  1.71 us

profile of v3, /device:TPU:1, one launch (start us, length us, event | category | flops | bytes accessed | tf_op | source)
XLA Modules:
  0.0 80.2 jit_solution(6352079509690777421)
XLA Ops:
  0.6 77.9 %shard_map.85 = (bf16[512,256]{1,0:T(8,128)(2,1)}, f32[32,256]{1,0:T(8,128)}, f32[32,256]{1,0:T(8,128)}) custom-call(bf16[3072,256]{1,0:T(8,128)(2,1)} %tok.1, bf16[3072,256]{1,0:T(8,128)(2,1)} %cot.1, bf16[256,512]{1,0:T(8,128)(2,1)} %proj_hbm.1, bf16[512,256]{1,0:T(8,128)(2,1)} %wgt_hbm.1, f32[32,256]{1,0:T(8,128)} %m1_hbm.1, f32[32,256]{1,0:T(8,128)} %m2_hbm.1), custom_call_target="tpu_custom_call" | custom-call | flops 1800000000 | bytes 4500000 | tf_op jit(solution)/shard_map/pallas_call | solution.py:345
  78.5 1.7 %shard_map.86 = (bf16[512,256]{1,0:T(8,128)(2,1)}, f32[32,256]{1,0:T(8,128)}, f32[32,256]{1,0:T(8,128)}) custom-call(bf16[512,256]{1,0:T(8,128)(2,1)} %get-tuple-element.6.nw, f32[32,256]{1,0:T(8,128)} %get-tuple-element.7.n1, f32[32,256]{1,0:T(8,128)} %get-tuple-element.8.n2), custom_call_target="tpu_custom_call" | custom-call | tf_op jit(solution)/shard_map/pallas_call | solution.py:356

commit v4 on v3

--- a/solution.py
+++ b/solution.py
@@ -17,7 +17,7 @@
 RANK = 512
 WIDTH = 256
 QUARTER = 768
-SIZES = (256, 256, 256)
+SIZES = (128, 256, 256, 128)
 CHUNKS = len(SIZES)
 STARTS = tuple(sum(SIZES[:k]) for k in range(CHUNKS))
 MESH = pl.DeviceIdType.MESH
@@ -55,21 +55,14 @@
         cp.start()
         sent.append(cp)
 
+    def drain(keep=0):
+        while len(sent) > keep:
+            sent.pop(0).wait_send()
+
     def got(dst, sem):
         pltpu.make_async_remote_copy(
             src_ref=dst, dst_ref=dst, send_sem=s_out, recv_sem=sem, device_id=(dp, fs), device_id_type=MESH
         ).wait_recv()
-
-    own_t = pltpu.make_async_copy(tok.at[pl.ds(x * QUARTER, QUARTER)], t4.at[0], lsem.at[0])
-    own_c = pltpu.make_async_copy(cot.at[pl.ds(x * QUARTER, QUARTER)], c4.at[0], lsem.at[1])
-    loads = [
-        pltpu.make_async_copy(src, dst, lsem.at[i + 2])
-        for i, (src, dst) in enumerate(((proj_hbm, proj), (wgt_hbm, wgt), (m1_hbm, m1), (m2_hbm, m2)))
-    ]
-    for load in loads:
-        load.start()
-    own_t.start()
-    own_c.start()
 
     barrier = pltpu.get_barrier_semaphore()
     for d in range(1, NX):
@@ -80,6 +73,22 @@
         pl.semaphore_signal(barrier, inc=1, device_id=py(d, True), device_id_type=MESH)
         if d:
             pl.semaphore_signal(barrier, inc=1, device_id=py(d), device_id_type=MESH)
+    own_t = pltpu.make_async_copy(tok.at[x], t4.at[0], lsem.at[0])
+    own_c = pltpu.make_async_copy(cot.at[x], c4.at[0], lsem.at[1])
+    loads = [
+        pltpu.make_async_copy(src, dst, lsem.at[i + 2])
+        for i, (src, dst) in enumerate(((proj_hbm, proj), (wgt_hbm, wgt), (m1_hbm, m1), (m2_hbm, m2)))
+    ]
+    for load in loads:
+        load.start()
+    own_t.start()
+    own_c.start()
+
+    def send_tok(k):
+        rows = pl.ds(STARTS[k], SIZES[k])
+        for d in (2, 1, 3):
+            put(tok.at[lax.rem(x + d, NX), rows], t4.at[d, rows], s_t.at[k], px(d))
+
     loads[0].wait()
     pt[0] = proj[...].T
     pu1[x] = proj[pl.ds(dp * 16, 16)]
@@ -94,9 +103,7 @@
     for d in (2, 1, 3):
         put(pu1.at[x], pu1.at[x], s_u1.at[0], px(d))
     for k in range(CHUNKS):
-        for d in (2, 1, 3):
-            rows = pl.ds(lax.rem(x + d, NX) * QUARTER + STARTS[k], SIZES[k])
-            put(tok.at[rows], t4.at[d, pl.ds(STARTS[k], SIZES[k])], s_t.at[k], px(d))
+        send_tok(k)
 
     got(pt.at[others, ranks(c, y)], s_pt.at[0])
     far = 2 - 4 * c
@@ -127,8 +134,8 @@
     def send_cot():
         for k in range(CHUNKS):
             for d in (2, 1, 3):
-                rows = pl.ds(lax.rem(x + d, NX) * QUARTER + STARTS[k], SIZES[k])
-                put(cot.at[rows], c4.at[d, pl.ds(STARTS[k], SIZES[k])], s_c.at[k], px(d))
+                rows = pl.ds(STARTS[k], SIZES[k])
+                put(cot.at[lax.rem(x + d, NX), rows], c4.at[d, rows], s_c.at[k], px(d))
 
     def at(d):
         return lax.rem(z + d + NZ, NZ)
@@ -206,6 +213,8 @@
     for k in range(CHUNKS):
         rows = pl.ds(STARTS[k], SIZES[k])
         got(ag[k].at[pl.ds(0, 5)], s_a.at[k, 1])
+        if k == CHUNKS - 1:
+            drain(3 * CHUNKS)
         got(c4.at[others, rows], s_c.at[k])
         low = ag[k][...].reshape(RANK, SIZES[k])
         for d in (2, 1, 3, 0):
@@ -235,6 +244,7 @@
         for slot in (1, 2):
             xs[h, slot - 1] = paired(h, slot).astype(BF16)
             put(xs.at[h, slot - 1], xr.at[h, slot - 1], s_x.at[h], px(-order[slot]))
+    drain(22)
     for h in halves:
         got(gc.at[h, groups[2]], s_g.at[h, 2])
         total = paired(h, 3)
@@ -244,6 +254,7 @@
         ys[h] = total.astype(BF16)
         for d in (4, 3, 5, 2, 6, 1, 7):
             put(ys.at[h, lax.rem(y + d, NY)], yr.at[h, d], s_y.at[h], py(d))
+    drain(14)
     for h in halves:
         got(y2r.at[h, pl.ds(1, NY - 1)], s_y2.at[h])
         total = y2sum[h, y]
@@ -270,6 +281,7 @@
             put(dirb.at[y, c, h], dirb.at[y, c, h], s_d.at[h], py(d))
         n1[rows] = new_first
         n2[rows] = new_second
+    drain(14)
     got(pu3.at[:, pl.ds(0, 2 * NY - 1)], s_u3.at[0])
     for h in halves:
         got(dirb.at[pl.ds(0, NY - 1), c, h], s_d.at[h])
@@ -280,20 +292,17 @@
         pu3[...].reshape(RANK, RANK), dirb[...].reshape(RANK, WIDTH), preferred_element_type=F32
     )
     nw[...] = (wgt[...].astype(F32) - RATE * update).astype(BF16)
-    for cp in sent:
-        cp.wait_send()
-
-
-def hand_over(nw, n1, n2, nw_out, n1_out, n2_out, a, b, e, sems):
-    trips = ((nw, a, nw_out), (n1, b, n1_out), (n2, e, n2_out))
-    ins = [pltpu.make_async_copy(src, mid, sems.at[0, i]) for i, (src, mid, _) in enumerate(trips)]
-    outs = [pltpu.make_async_copy(mid, dst, sems.at[1, i]) for i, (_, mid, dst) in enumerate(trips)]
-    for copy in ins:
+    drain()
+
+
+def hand_over(nw, n1, n2, nw_out, n1_out, n2_out, sems):
+    copies = [
+        pltpu.make_async_copy(src, dst, sems.at[i])
+        for i, (src, dst) in enumerate(((nw, nw_out), (n1, n1_out), (n2, n2_out)))
+    ]
+    for copy in copies:
         copy.start()
-    for first, second in zip(ins, outs):
-        first.wait()
-        second.start()
-    for copy in outs:
+    for copy in copies:
         copy.wait()
 
 
@@ -344,7 +353,7 @@
     )
     results = pl.pallas_call(
         kernel,
-        out_shape=shapes,
+        out_shape=tuple(v(t.shape, t.dtype) for t in shapes),
         in_specs=[hbm] * 6,
         out_specs=(vmem, vmem, vmem),
         scratch_shapes=scratch,
@@ -352,15 +361,14 @@
             collective_id=0, has_side_effects=True, vmem_limit_bytes=63 * 2**20
         ),
         cost_estimate=pl.CostEstimate(flops=1_800_000_000, bytes_accessed=4_500_000, transcendentals=8192),
-    )(tokens, cotangent, projection, weight, first_moment, second_moment)
+    )(*(a.reshape(NX, QUARTER, WIDTH) for a in (tokens, cotangent)), projection, weight, first_moment, second_moment)
     return pl.pallas_call(
         hand_over,
         out_shape=shapes,
-        in_specs=[hbm] * 3,
+        in_specs=[vmem] * 3,
         out_specs=(hbm, hbm, hbm),
-        scratch_shapes=[v(t.shape, t.dtype) for t in shapes] + [dma((2, 3))],
-        compiler_params=pltpu.CompilerParams(vmem_limit_bytes=63 * 2**20),
-    )(*results)
+        scratch_shapes=[dma((3,))],
+    )(*(pltpu.with_memory_space_constraint(r, pltpu.VMEM) for r in results))
 
 
 def solution(mesh):

time: 80.4 us -> 78.3 us (0.974)
  Pallas kernels: 79.6 us -> 77.6 us
    pallas_call x2, Pallas kernels: 79.6 us -> 77.6 us  [the longest x1 76.8 us: shards(): pl.pallas_call(kernel, out_shape=tuple((v(t.shape, t.dtype) for t in shap...]
where the time goes in v4:
time: 78.3 us; the launch traced here: 78.2 us
  Pallas kernels  77.6 us (99%)
    pallas_call x1, Pallas kernels, shards(): pl.pallas_call(kernel, out_shape=tuple((v(t.shape, t.dtype) for t in shap...  76.8 us

profile of v4, /device:TPU:1, one launch (start us, length us, event | category | flops | bytes accessed | tf_op | source)
XLA Modules:
  0.0 78.2 jit_solution(10565362525041847338)
XLA Ops:
  0.6 76.8 %shard_map.85 = (bf16[512,256]{1,0:T(8,128)(2,1)S(1)}, f32[32,256]{1,0:T(8,128)S(1)}, f32[32,256]{1,0:T(8,128)S(1)}) custom-call(bf16[4,768,256]{2,1,0:T(8,128)(2,1)} %bitcast.2, bf16[4,768,256]{2,1,0:T(8,128)(2,1)} %bitcast.3, bf16[256,512]{1,0:T(8,128)(2,1)} %proj_hbm.1, bf16[512,256]{1,0:T(8,128)(2,1)} %wgt_hbm.1, f32[32,256]{1,0:T(8,128)} %m1_hbm.1, ...), custom_call_target="tpu_custom_call" | custom-call | flops 1800000000 | bytes 4500000 | tf_op jit(solution)/shard_map/pallas_call | solution.py:354
  77.5 0.7 shard_map.86

commit v5 on v4

--- a/solution.py
+++ b/solution.py
@@ -19,6 +19,8 @@
 QUARTER = 768
 SIZES = (128, 256, 256, 128)
 CHUNKS = len(SIZES)
+SUM_AT_ONCE = ()
+GATHER_AT_ONCE = (CHUNKS - 1,)
 STARTS = tuple(sum(SIZES[:k]) for k in range(CHUNKS))
 MESH = pl.DeviceIdType.MESH
 F32 = jnp.float32
@@ -154,11 +156,17 @@
             low = part if low is None else low + part
         psend[k][...] = low.astype(BF16).reshape(NZ, RANK // NZ, SIZES[k])
         e = sign(k)
+        if k in SUM_AT_ONCE:
+            for d in (4, 3, 5, 2, 6, 1, 7):
+                put(psend[k].at[at(d)], zr[k].at[d], s_z.at[k, 1], pz(d))
+            return
         for owner, to, slot in ((-4, -e, 0), (-2 * e, e, 1), (e, -e, 2), (3 * e, e, 3), (-e, -e, 4)):
             put(psend[k].at[at(owner)], zr[k].at[slot], s_z.at[k, slot // 4], pz(to))
 
     def middle(k):
         e = sign(k)
+        if k in SUM_AT_ONCE:
+            return
         got(zr[k].at[pl.ds(0, 4)], s_z.at[k, 0])
         for owner, one, two, slot in ((-3 * e, 0, 1, 5), (2 * e, 2, 3, 6)):
             both = zr[k][one].astype(F32) + zr[k][two].astype(F32)
@@ -168,15 +176,22 @@
     def reduce(k):
         e = sign(k)
         total = psend[k][z].astype(F32)
-        got(zr[k].at[pl.ds(4, 3)], s_z.at[k, 1])
-        for slot in (4, 5, 6):
+        slots = range(1, NZ) if k in SUM_AT_ONCE else range(4, 7)
+        got(zr[k].at[pl.ds(slots[0], len(slots))], s_z.at[k, 1])
+        for slot in slots:
             total = total + zr[k][slot].astype(F32)
         ag[k][z] = total.astype(BF16)
+        if k in GATHER_AT_ONCE:
+            for d in (4, 3, 5, 2, 6, 1, 7):
+                put(ag[k].at[z], ag[k].at[z], s_a.at[k, 1], pz(d))
+            return
         for d in (3 * e, -2 * e, e):
             put(ag[k].at[z], ag[k].at[z], s_a.at[k, 1 if d == e else 0], pz(d))
 
     def forward(k):
         e = sign(k)
+        if k in GATHER_AT_ONCE:
+            return
         got(ag[k].at[pl.ds(0, 2)], s_a.at[k, 0])
         for d in (-2 * e, 3 * e):
             for f in (e, -e):
@@ -212,7 +227,7 @@
     own_c.wait()
     for k in range(CHUNKS):
         rows = pl.ds(STARTS[k], SIZES[k])
-        got(ag[k].at[pl.ds(0, 5)], s_a.at[k, 1])
+        got(ag[k].at[pl.ds(0, 7 if k in GATHER_AT_ONCE else 5)], s_a.at[k, 1])
         if k == CHUNKS - 1:
             drain(3 * CHUNKS)
         got(c4.at[others, rows], s_c.at[k])

time: 78.3 us -> 76.1 us (0.972)
  Pallas kernels: 77.6 us -> 75.3 us
    pallas_call x1, Pallas kernels: 76.8 us -> 74.5 us  [shards(): pl.pallas_call(kernel, out_shape=tuple((v(t.shape, t.dtype) for t in shap...]
where the time goes in v5:
time: 76.1 us; the launch traced here: 75.9 us
  Pallas kernels  75.3 us (99%)
    pallas_call x1, Pallas kernels, shards(): pl.pallas_call(kernel, out_shape=tuple((v(t.shape, t.dtype) for t in shap...  74.5 us

profile of v5, /device:TPU:1, one launch (start us, length us, event | category | flops | bytes accessed | tf_op | source)
XLA Modules:
  0.0 75.9 jit_solution(10708448683851810226)
XLA Ops:
  0.6 74.5 %shard_map.85 = (bf16[512,256]{1,0:T(8,128)(2,1)S(1)}, f32[32,256]{1,0:T(8,128)S(1)}, f32[32,256]{1,0:T(8,128)S(1)}) custom-call(bf16[4,768,256]{2,1,0:T(8,128)(2,1)} %bitcast.2, bf16[4,768,256]{2,1,0:T(8,128)(2,1)} %bitcast.3, bf16[256,512]{1,0:T(8,128)(2,1)} %proj_hbm.1, bf16[512,256]{1,0:T(8,128)(2,1)} %wgt_hbm.1, f32[32,256]{1,0:T(8,128)} %m1_hbm.1, ...), custom_call_target="tpu_custom_call" | custom-call | flops 1800000000 | bytes 4500000 | tf_op jit(solution)/shard_map/pallas_call | solution.py:369
  75.2 0.7 shard_map.86

commit v6 on v5

--- a/solution.py
+++ b/solution.py
@@ -208,7 +208,7 @@
                 else:
                     put(src, pu3.at[:, dp], s_u3.at[0], py(d, e == 1))
 
-    for k in range(CHUNKS + 3):
+    for k in range(CHUNKS + 4):
         if k < CHUNKS:
             partial(k)
         if k == CHUNKS - 2:
@@ -217,8 +217,8 @@
             middle(k - 1)
         if 0 <= k - 2 < CHUNKS:
             reduce(k - 2)
-        if 0 <= k - 3 < CHUNKS:
-            forward(k - 3)
+        if 0 <= k - 4 < CHUNKS:
+            forward(k - 4)
         if k < 2:
             relay(k + 3)
         if k == 2:

time: 76.1 us -> 75.8 us (level)
  no operation moved by 1% of the time
where the time goes in v6:
time: 75.8 us; the launch traced here: 75.7 us
  Pallas kernels  75 us (99%)
    pallas_call x1, Pallas kernels, shards(): pl.pallas_call(kernel, out_shape=tuple((v(t.shape, t.dtype) for t in shap...  74.3 us

profile of v6, /device:TPU:1, one launch (start us, length us, event | category | flops | bytes accessed | tf_op | source)
XLA Modules:
  0.0 75.7 jit_solution(857910515286841428)
XLA Ops:
  0.6 74.3 %shard_map.85 = (bf16[512,256]{1,0:T(8,128)(2,1)S(1)}, f32[32,256]{1,0:T(8,128)S(1)}, f32[32,256]{1,0:T(8,128)S(1)}) custom-call(bf16[4,768,256]{2,1,0:T(8,128)(2,1)} %bitcast.2, bf16[4,768,256]{2,1,0:T(8,128)(2,1)} %bitcast.3, bf16[256,512]{1,0:T(8,128)(2,1)} %proj_hbm.1, bf16[512,256]{1,0:T(8,128)(2,1)} %wgt_hbm.1, f32[32,256]{1,0:T(8,128)} %m1_hbm.1, ...), custom_call_target="tpu_custom_call" | custom-call | flops 1800000000 | bytes 4500000 | tf_op jit(solution)/shard_map/pallas_call | solution.py:369
  74.9 0.7 shard_map.86
